TPU v7x, 512 devices: a whole 4x4x16 slice. The times are simulated.
512 devices in a mesh: seq: 16 (over y, x), blk: 16 (over z_lo, core), cfg: 2 (over z_hi).
Axes of the slice: x: 4, y: 4, z: 16 (z_hi: 2, z_lo: 8; z = z_hi * 8 + z_lo), core: 2. Of those that a mesh axis runs over, the one named last changes fastest.
Arguments:
- queries: bfloat16 [2, 8192, 4096], P('cfg', ('seq', 'blk')), may hold values from -6 to 6
- keys: bfloat16 [2, 8192, 4096], P('cfg', ('seq', 'blk')), may hold values from -6 to 6
- values: bfloat16 [2, 8192, 4096], P('cfg', ('seq', 'blk')), may hold values from -6 to 6
- head_weight: bfloat16 [4096, 64], replicated, may hold values from -0.09375 to 0.09375
- noisy_latent: float32 [16, 32, 64, 16], P('seq', 'blk', 'cfg'), may hold values from -6 to 6
- noise_level: float32 [1], replicated, may hold values from 0.3 to 1
- conv_weight: bfloat16 [3, 3, 3, 16, 384], replicated, may hold values from -0.3125 to 0.3125
Outputs:
- clean_latent: float32 [16, 32, 64, 16], P('seq', 'blk', 'cfg')
- decoded: bfloat16 [16, 32, 64, 384], P('seq', 'blk', 'cfg')
All inputs are finite; a program needn't handle non-finite values.
Results may differ from a plain program's by a relative error of at most 0.013.
Values may be sent and summed in bfloat16 or wider, within the bound.
A program may use at most 64 MiB of HBM per device.

v0:
```python
import math

import jax
import jax.numpy as jnp
from jax import lax
from jax.sharding import PartitionSpec as P

HEAD_DIM = 128


guide_scale = 5.0
norm_eps = 1e-06


def padded(shard, sides, width):
    for axis, dim in sides:
        size, length = (lax.axis_size(axis), shard.shape[dim])
        up = [(i, (i + 1) % size) for i in range(size - 1)]
        down = [(j, i) for i, j in up]
        last = lax.slice_in_dim(shard, length - width, length, axis=dim)
        initial = lax.slice_in_dim(shard, 0, width, axis=dim)
        before = lax.ppermute(last, axis, up)
        after = lax.ppermute(initial, axis, down)
        shard = jnp.concatenate([before, shard, after], axis=dim)
    return shard


def passed_along(value, axis, steps):
    count = lax.axis_size(axis)
    initial, last = (max(0, -steps), min(count, count - steps))
    return lax.ppermute(value, axis, [(source, source + steps) for source in range(initial, last)])


def prepare(query_part):
    count = query_part.shape[1]
    query = query_part[0].reshape(count, -1, HEAD_DIM)
    heads = query.shape[1]
    scale = HEAD_DIM ** (-0.5)

    def fold(state, piece, start):
        key_part, value_part = piece
        rows = key_part.shape[1]
        step_rows = math.gcd(rows, 1024)
        key_blocks = key_part[0].reshape(rows // step_rows, step_rows, heads, HEAD_DIM)
        value_blocks = value_part[0].reshape(rows // step_rows, step_rows, heads, HEAD_DIM)

        def one_block(carry, pair):
            largest, total, summed = carry
            key_block, value_block = pair
            scores = (
                jnp.einsum("qhd,khd->hqk", query, key_block, preferred_element_type=jnp.float32)
                * scale
            )
            fresh = jnp.maximum(largest, jnp.max(scores, axis=-1))
            factor = jnp.exp(largest - fresh)
            probs = jnp.exp(scores - fresh[..., None])
            total = total * factor + jnp.sum(probs, axis=-1)
            mixed = jnp.einsum(
                "hqk,khd->qhd",
                probs.astype(jnp.bfloat16),
                value_block,
                preferred_element_type=jnp.float32,
            )
            summed = summed * factor.T[..., None] + mixed
            return ((fresh, total, summed), None)

        state, unused = lax.scan(one_block, state, (key_blocks, value_blocks))
        return state

    start_state = (
        jnp.full((heads, count), -1e30, jnp.float32),
        jnp.zeros((heads, count), jnp.float32),
        jnp.zeros((count, heads, HEAD_DIM), jnp.float32),
    )
    return (fold, start_state)


def finish(state):
    largest, total, summed = state
    attended = (summed / total.T[..., None]).astype(jnp.bfloat16)
    return attended.reshape(1, attended.shape[0], -1)


def convolve(stack, conv_weight):
    rows = stack.shape[1] - 2
    cols = stack.shape[2] - 2
    channels = stack.shape[3]
    taps = []
    for offset_f in range(3):
        for offset_r in range(3):
            for offset_c in range(3):
                taps.append(
                    stack[offset_f, offset_r : offset_r + rows, offset_c : offset_c + cols, :]
                )
    patches = jnp.concatenate(taps, axis=-1).reshape(rows * cols, 27 * channels)
    kernel = conv_weight.reshape(27 * channels, conv_weight.shape[4])
    summed = jnp.dot(patches, kernel, preferred_element_type=jnp.float32)
    factor = lax.rsqrt(jnp.mean(summed * summed, axis=-1, keepdims=True) + norm_eps)
    decoded = jax.nn.silu(summed * factor).astype(jnp.bfloat16)
    return decoded.reshape(1, rows, cols, conv_weight.shape[4])


def local(queries, keys, values, head_weight, noisy_latent, noise_level, conv_weight):
    query_part, key_part, value_part = (
        lax.all_to_all(queries, "seq", split_axis=2, concat_axis=1, tiled=True),
        lax.all_to_all(keys, "seq", split_axis=2, concat_axis=1, tiled=True),
        lax.all_to_all(values, "seq", split_axis=2, concat_axis=1, tiled=True),
    )
    fold, start_state = prepare(query_part)
    state = fold(
        start_state,
        (
            lax.all_gather(key_part, "blk", axis=1, tiled=True),
            lax.all_gather(value_part, "blk", axis=1, tiled=True),
        ),
        jnp.int32(0),
    )
    branches = lax.all_to_all(
        lax.all_to_all(finish(state), "seq", split_axis=1, concat_axis=2, tiled=True),
        "cfg",
        split_axis=1,
        concat_axis=0,
        tiled=True,
    )
    cond = branches[0].astype(jnp.float32)
    uncond = branches[1].astype(jnp.float32)
    guided = uncond + guide_scale * (cond - uncond)
    velocity = jnp.dot(guided, head_weight.astype(jnp.float32), precision=lax.Precision.HIGHEST)
    half = velocity.shape[0]
    channels = noisy_latent.shape[3]
    motion = (
        velocity.reshape(half, 2, 2, channels)
        .transpose(1, 0, 2, 3)
        .reshape(1, 2, 2 * half, channels)
    )
    clean_latent = noisy_latent - noise_level[0] * motion
    tile = clean_latent.astype(jnp.bfloat16)
    framed = padded(tile, (("blk", 1), ("cfg", 2)), 1)
    frames = [framed]
    for repeat in range(2):
        frames.insert(0, passed_along(frames[0], "seq", 1))
    stack = jnp.concatenate(frames, axis=0)
    decoded = convolve(stack, conv_weight)
    return (clean_latent, decoded)


def solution(mesh):
    in_specs = (
        P("cfg", ("seq", "blk"), None),
        P("cfg", ("seq", "blk"), None),
        P("cfg", ("seq", "blk"), None),
        P(),
        P("seq", "blk", "cfg", None),
        P(),
        P(),
    )
    out_specs = (P("seq", "blk", "cfg", None), P("seq", "blk", "cfg", None))
    return jax.shard_map(local, mesh=mesh, in_specs=in_specs, out_specs=out_specs, check_vma=False)
```

profile of v0, /device:TPU:24, one launch (start us, length us, event | category | flops | bytes accessed | tf_op | source)
XLA Modules:
  0.0 444.2 jit_solution(8885952635678395038)
XLA Ops:
  7.2 4.5 %copy.145 = bf16[1,32,4096]{1,0,2:T(2,128)(2,1)S(1)} copy(bf16[1,32,4096]{2,1,0:T(8,128)(2,1)} %param.10) | data formatting | bytes 524288 | tf_op args[1]
  12.3 23.4 %reduce = bf16[4096,32]{1,0:T(8,128)(2,1)} reduce(bf16[4096,1,32]{2,1,0:T(2,128)(2,1)S(1)} %bitcast.173, bf16[]{:T(256)} %broadcast.78), dimensions={1}, to_apply=%bitcast.133.reduce_sub_computation | reduce | bytes 524290
  38.2 14.5 %all_to_all.82 = bf16[16,2,4096]{2,1,0:T(2,128)(2,1)S(1)} all-to-all(bf16[16,2,4096]{2,1,0:T(2,128)(2,1)S(1)} %reshape.125), channel_id=1, replica_groups=mesh['seq'=16,'blk'=16,'cfg'=2] {'seq'}, dimensions={0} | all-to-all | bytes 524288 | tf_op jit(solution)/shard_map/all_to_all | solution.py:106
  60.0 23.4 %reduce.2 = bf16[4096,32]{1,0:T(8,128)(2,1)} reduce(bf16[4096,1,32]{2,1,0:T(2,128)(2,1)S(1)} %bitcast.174, bf16[]{:T(256)} %broadcast.78), dimensions={1}, to_apply=%bitcast.137.reduce_sub_computation | reduce | bytes 524290
  85.9 11.6 %all_to_all.83 = bf16[16,2,4096]{2,1,0:T(2,128)(2,1)S(1)} all-to-all(bf16[16,2,4096]{2,1,0:T(2,128)(2,1)S(1)} %reshape.129), channel_id=1, replica_groups=mesh['seq'=16,'blk'=16,'cfg'=2] {'seq'}, dimensions={0} | all-to-all | bytes 524288 | tf_op jit(solution)/shard_map/all_to_all | solution.py:107
  104.6 23.5 %reduce.1 = bf16[4096,32]{1,0:T(8,128)(2,1)} reduce(bf16[4096,1,32]{2,1,0:T(2,128)(2,1)S(1)} %bitcast.175, bf16[]{:T(256)} %broadcast.78), dimensions={1}, to_apply=%bitcast.135.reduce_sub_computation | reduce | bytes 524290
  131.2 5.8 %all-to-all-start.1 = ((bf16[16,2,4096]{2,1,0:T(2,128)(2,1)}), bf16[16,2,4096]{2,1,0:T(2,128)(2,1)S(1)}, u32[]{:S(2)}, u32[]{:S(2)}) async-start(bf16[16,2,4096]{2,1,0:T(2,128)(2,1)} %reshape.127), calls=%async_computation.1 | async-start | bytes 524288 | tf_op jit(solution)/shard_map/all_to_all | solution.py:105
  137.0 6.4 %all-to-all-done.1 = bf16[16,2,4096]{2,1,0:T(2,128)(2,1)S(1)} async-done(((bf16[16,2,4096]{2,1,0:T(2,128)(2,1)}), bf16[16,2,4096]{2,1,0:T(2,128)(2,1)S(1)}, u32[]{:S(2)}, u32[]{:S(2)}) %all-to-all-start.1) | async-done | bytes 262176 | tf_op jit(solution)/shard_map/all_to_all | solution.py:105
  147.1 18.2 %all-gather.3.cloned.1.call-done = bf16[1,8192,256]{2,1,0:T(8,128)(2,1)} async-done(((bf16[1,512,256]{2,1,0:T(8,128)(2,1)}), bf16[1,8192,256]{2,1,0:T(8,128)(2,1)}) %all-gather.3.cloned.1.call-update) | async-done | bytes 4194320 | tf_op jit(solution)/shard_map/all_gather | solution.py:113
  165.2 6.9 %reshape.122 = bf16[8,1024,2,128]{3,2,1,0:T(2,128)(2,1)} reshape(bf16[1,8192,256]{2,1,0:T(8,128)(2,1)} %all-gather.3.cloned.1.call-done) | data formatting | bytes 8388608 | tf_op jit(solution)/shard_map/reshape;squeeze | solution.py:44
  172.2 100.0 %all-gather.5.cloned.1.call-done = bf16[1,8192,256]{2,1,0:T(8,128)(2,1)} async-done(((bf16[1,512,256]{2,1,0:T(8,128)(2,1)}), bf16[1,8192,256]{2,1,0:T(8,128)(2,1)}) %all-gather.5.cloned.1.call-update) | async-done | bytes 4194320 | tf_op jit(solution)/shard_map/all_gather | solution.py:114
  272.2 6.9 %reshape.123 = bf16[8,1024,2,128]{3,2,1,0:T(2,128)(2,1)} reshape(bf16[1,8192,256]{2,1,0:T(8,128)(2,1)} %all-gather.5.cloned.1.call-done) | data formatting | bytes 8388608 | tf_op jit(solution)/shard_map/reshape;squeeze | solution.py:45
  279.1 74.1 %while.15 = (s32[]{:T(128)}, f32[2,512]{1,0:T(2,128)S(1)}, f32[2,512]{1,0:T(2,128)S(1)}, f32[512,2,128]{0,2,1:T(8,128)S(1)}, bf16[8,1024,2,128]{3,2,1,0:T(2,128)...) while((s32[]{:T(128)}, f32[2,512]{1,0:T(2,128)S(1)}, ...), condition=%wide.region_3.4_spmd.clone, body=%wide.region_0.3_spmd.clone.sunk | while | flops 545658880 | bytes 34930824 | solution.py:67
  293.4 3.3 fusion.51
  311.9 3.3 fusion.51
  321.2 3.3 fusion.51
  330.5 3.3 fusion.51
  349.0 3.3 fusion.51
  356.0 13.6 %all_to_all.84 = bf16[16,2,4096]{2,1,0:T(2,128)(2,1)S(1)} all-to-all(bf16[16,2,4096]{2,1,0:T(2,128)(2,1)S(1)} %reshape.131), channel_id=1, replica_groups=mesh['seq'=16,'blk'=16,'cfg'=2] {'seq'}, dimensions={0} | all-to-all | bytes 524288 | tf_op jit(solution)/shard_map/all_to_all | solution.py:119
  373.3 8.8 %all-to-all-start.4 = ((bf16[2,2,32768]{2,1,0:T(2,128)(2,1)}), bf16[2,2,32768]{2,1,0:T(2,128)(2,1)S(1)}, u32[]{:S(2)}, u32[]{:S(2)}) async-start(bf16[2,2,32768]{2,1,0:T(2,128)(2,1)} %reshape.133), calls=%async_computation.4 | async-start | bytes 524288 | tf_op jit(solution)/shard_map/all_to_all | solution.py:118
  382.8 13.2 %all-to-all-done.4 = bf16[2,2,32768]{2,1,0:T(2,128)(2,1)S(1)} async-done(((bf16[2,2,32768]{2,1,0:T(2,128)(2,1)}), bf16[2,2,32768]{2,1,0:T(2,128)(2,1)S(1)}, u32[]{:S(2)}, u32[]{:S(2)}) %all-to-all-start.4) | async-done | bytes 262176 | tf_op jit(solution)/shard_map/all_to_all | solution.py:118
  406.7 12.6 %collective-permute-done.3 = bf16[1,4,1,16]{3,2,1,0:T(2,128)(2,1)S(1)} collective-permute-done((bf16[1,4,1,16]{3,2,1,0:T(2,128)(2,1)S(1)}, bf16[1,4,1,16]{3,2,1,0:T(2,128)(2,1)S(1)}, u32[]{:S(2)}, u32[]{:S(2)}) %collective-permute-start.3) | collective-permute-done | bytes 160 | tf_op jit(solution)/shard_map/ppermute | solution.py:23
  422.7 4.6 %collective-permute-done.4 = bf16[1,4,34,16]{2,3,1,0:T(8,128)(2,1)S(1)} collective-permute-done((bf16[1,4,34,16]{2,3,1,0:T(8,128)(2,1)S(1)}, bf16[1,4,34,16]{2,3,1,0:T(8,128)(2,1)S(1)}, u32[]{:S(2)}, u32[]{:S(2)}) %collective-permute-start.4) | collective-permute-done | bytes 4384 | tf_op jit(solution)/shard_map/ppermute | solution.py:31
  430.1 4.8 %collective-permute-done.5 = bf16[1,4,34,16]{2,3,1,0:T(8,128)(2,1)S(1)} collective-permute-done((bf16[1,4,34,16]{2,3,1,0:T(8,128)(2,1)S(1)}, bf16[1,4,34,16]{2,3,1,0:T(8,128)(2,1)S(1)}, u32[]{:S(2)}, u32[]{:S(2)}) %collective-permute-start.5) | collective-permute-done | bytes 4384 | tf_op jit(solution)/shard_map/ppermute | solution.py:31
  (233 shorter events, 109.3 us)
Async XLA Ops:
  7.2 389.6 %copy-start = (bf16[4096,64]{0,1:T(8,128)(2,1)S(1)}, bf16[4096,64]{0,1:T(8,128)(2,1)}, u32[]{:S(2)}) copy-start(bf16[4096,64]{0,1:T(8,128)(2,1)} %param.12) | copy-start | bytes 1572868
  7.2 158.1 %all-gather.3.cloned.1.call-start = ((), (), s32[]{:S(2)}) async-start(), calls=%async_computation.5 | async-start | bytes 4456448 | tf_op jit(solution)/shard_map/all_gather | solution.py:113
  35.7 21.6 %copy-start.3 = (bf16[1,32,4096]{2,1,0:T(8,128)(2,1)S(1)}, bf16[1,32,4096]{2,1,0:T(8,128)(2,1)}, u32[]{:S(2)}) copy-start(bf16[1,32,4096]{2,1,0:T(8,128)(2,1)} %param.11) | copy-start | bytes 786436
  57.0 215.2 %all-gather.5.cloned.1.call-start = ((), (), s32[]{:S(2)}) async-start(), calls=%async_computation.6 | async-start | bytes 4456448 | tf_op jit(solution)/shard_map/all_gather | solution.py:114
  83.4 18.5 %copy-start.4 = (bf16[1,32,4096]{2,1,0:T(8,128)(2,1)S(1)}, bf16[1,32,4096]{2,1,0:T(8,128)(2,1)}, u32[]{:S(2)}) copy-start(bf16[1,32,4096]{2,1,0:T(8,128)(2,1)} %param.9) | copy-start | bytes 786436
  131.2 12.2 %all-to-all-start.1 = ((bf16[16,2,4096]{2,1,0:T(2,128)(2,1)}), bf16[16,2,4096]{2,1,0:T(2,128)(2,1)S(1)}, u32[]{:S(2)}, u32[]{:S(2)}) async-start(bf16[16,2,4096]{2,1,0:T(2,128)(2,1)} %reshape.127), calls=%async_computation.1 | async-start | bytes 524288 | tf_op jit(solution)/shard_map/all_to_all | solution.py:105
  284.1 3.5 copy-start.1
  293.4 3.5 copy-start.1
  302.7 3.5 copy-start.1
  311.9 3.5 copy-start.1
  321.2 3.5 copy-start.1
  330.4 3.5 copy-start.1
  339.7 3.5 copy-start.1
  349.0 3.5 copy-start.1
  353.2 29.6 %copy-start.5 = (f32[1,2,32,16]{2,3,1,0:T(8,128)S(1)}, f32[1,2,32,16]{2,3,1,0:T(8,128)}, u32[]{:S(2)}) copy-start(f32[1,2,32,16]{2,3,1,0:T(8,128)} %param.13) | copy-start | bytes 12292
  369.9 66.4 %copy-start.2 = (bf16[3,3,3,16,384]{4,3,2,1,0:T(8,128)(2,1)S(1)}, bf16[3,3,3,16,384]{4,3,2,1,0:T(8,128)(2,1)}, u32[]{:S(2)}) copy-start(bf16[3,3,3,16,384]{4,3,2,1,0:T(8,128)(2,1)} %param.15) | copy-start | bytes 995332
  373.3 22.8 %all-to-all-start.4 = ((bf16[2,2,32768]{2,1,0:T(2,128)(2,1)}), bf16[2,2,32768]{2,1,0:T(2,128)(2,1)S(1)}, u32[]{:S(2)}, u32[]{:S(2)}) async-start(bf16[2,2,32768]{2,1,0:T(2,128)(2,1)} %reshape.133), calls=%async_computation.4 | async-start | bytes 524288 | tf_op jit(solution)/shard_map/all_to_all | solution.py:118
  398.8 3.4 collective-permute-start
  400.1 3.1 collective-permute-start.1
  403.3 3.3 collective-permute-start.2
  405.1 14.2 %collective-permute-start.3 = (bf16[1,4,1,16]{3,2,1,0:T(2,128)(2,1)S(1)}, bf16[1,4,1,16]{3,2,1,0:T(2,128)(2,1)S(1)}, u32[]{:S(2)}, u32[]{:S(2)}) collective-permute-start(bf16[1,4,1,16]{3,2,1,0:T(2,128)(2,1)S(1)} %get-tuple-element.131), channel_id=1, source_target_pairs={{1,0},{3,2},{5,4},{7,6},{9,8},{11,10},{13,12},{15,14},{17,16},{19,... | collective-permute-start | bytes 392 | tf_op jit(solution)/shard_map/ppermute | solution.py:23
  419.5 7.7 %collective-permute-start.4 = (bf16[1,4,34,16]{2,3,1,0:T(8,128)(2,1)S(1)}, bf16[1,4,34,16]{2,3,1,0:T(8,128)(2,1)S(1)}, u32[]{:S(2)}, u32[]{:S(2)}) collective-permute-start(bf16[1,4,34,16]{2,3,1,0:T(8,128)(2,1)S(1)} %pad_maximum_fusion.3), channel_id=1, source_target_pairs={{0,32},{32,64},{64,96},{96,128},{128,160},{160,192},{192,224},{224... | collective-permute-start | bytes 13064 | tf_op jit(solution)/shard_map/ppermute | solution.py:31
  427.3 7.7 %collective-permute-start.5 = (bf16[1,4,34,16]{2,3,1,0:T(8,128)(2,1)S(1)}, bf16[1,4,34,16]{2,3,1,0:T(8,128)(2,1)S(1)}, u32[]{:S(2)}, u32[]{:S(2)}) collective-permute-start(bf16[1,4,34,16]{2,3,1,0:T(8,128)(2,1)S(1)} %collective-permute-done.4), channel_id=1, source_target_pairs={{0,32},{32,64},{64,96},{96,128},{128,160},{160,192},{192,224},{224... | collective-permute-start | bytes 13064 | tf_op jit(solution)/shard_map/ppermute | solution.py:31
Sparse Core Ops, SparseCore 0:
  57.1 108.0 all-gather.2
  167.3 104.8 all-gather.4
where the time goes:
time: 446 us; the launch traced here: 444 us
  waiting for transfers between devices  161 us (36%)
  other arithmetic  82 us (18%)
  local copies, waits for them, and re-layouts  71 us (16%)
  matrix products  50 us (11%)
  blocking collectives  39.7 us (9%)
  starting transfers between devices  24.9 us (6%)
  between operations  15.3 us (3%)
    all_gather x1, waiting for transfers between devices, local(): lax.all_gather(value_part, 'blk', axis=1, tiled=True)  100 us
    unnamed x8, other arithmetic  74.6 us
    dot_general x8, matrix products, one_block(): jnp.einsum('hqk,khd->qhd', probs.astype(jnp.bfloat16), value_block, prefe...  26.2 us
    unnamed x57, local copies, waits for them, and re-layouts  25.4 us
    dot_general x8, matrix products, one_block(): jnp.einsum('qhd,khd->hqk', query, key_block, preferred_element_type=jnp.f...  21.5 us
    dynamic_slice x16, local copies, waits for them, and re-layouts, fold(): state, unused = lax.scan(one_block, state, (key_blocks, value_blocks))  18.7 us
    all_gather x1, waiting for transfers between devices, local(): lax.all_gather(key_part, 'blk', axis=1, tiled=True)  18.2 us
    all_to_all x1, blocking collectives, local(): lax.all_to_all(keys, 'seq', split_axis=2, concat_axis=1, tiled=True)  14.5 us
  transfers between devices with their start and end apart: 10, of which 8 were waited for; matrix products, arithmetic and copies ran while one was open for 17% of the time, Pallas kernels for 0%

commit v1 on v0

v1 whole, which is shorter than its diff:
```python
import jax
import jax.numpy as jnp
from jax import lax
from jax.experimental import pallas as pl
from jax.experimental.pallas import tpu as pltpu
from jax.sharding import PartitionSpec as P

F32 = jnp.float32
BF16 = jnp.bfloat16
MESH = pl.DeviceIdType.MESH

guide_scale = 5.0
norm_eps = 1e-06
LOG_SCALE = float(128 ** (-0.5) * 1.4426950408889634)

NX = 4
NY = 4
NZ = 8
HEADS = 32
ROWS = 32
KV_ROWS = 48
V_ROWS = 80


def kernel(
    q_ref, k_ref, v_ref, w_ref, noisy_ref, level_ref, cw_ref,
    clean_ref, decoded_ref,
    send_kv, send_q, rkv, rq, vt, c1s, c1r, c2s, c2r, halo, ext, patches, moved,
    s_kv, s_q, r_kv, r_q, s_b1, r_b1, s_b2, r_b2, s_core, r_core,
    s_c1, r_c1, s_c2, r_c2, s_halo, r_halo,
):
    seq = lax.axis_index("seq")
    blk = lax.axis_index("blk")
    cfg = lax.axis_index("cfg")
    y, x = seq // NX, seq % NX
    z, core = blk // 2, blk % 2
    half, zl = z // 4, z % 4

    def from_plane(i):
        return ((half + i % 2) % 2) * 4 + (zl + 4 - i // 2) % 4

    def to_plane(i):
        return ((half + i % 2) % 2) * 4 + (zl + i // 2) % 4

    def group(yy, zz):
        return (yy * NX + x, zz * 2 + core, cfg)

    right = (y * NX + (x + 1) % NX, blk, cfg)
    left = (y * NX + (x + 3) % NX, blk, cfg)
    sibling = (seq, z * 2 + 1 - core, cfg)

    halo[...] = jnp.zeros_like(halo)
    ext[...] = jnp.zeros_like(ext)

    barrier = pltpu.get_barrier_semaphore()

    def greet(i, carry):
        zz, yy = to_plane(i // 4), (y + i % 4) % 4
        pl.semaphore_signal(barrier, inc=1, device_id=group(yy, zz), device_id_type=MESH)
        return carry

    lax.fori_loop(1, HEADS, greet, 0)
    for other in (right, left, sibling):
        pl.semaphore_signal(barrier, inc=1, device_id=other, device_id_type=MESH)

    def greet_branch(i, carry):
        pl.semaphore_signal(
            barrier, inc=1, device_id=(seq, i * 2 + core, 1 - cfg), device_id_type=MESH
        )
        return carry

    lax.fori_loop(0, NZ, greet_branch, 0)

    for h in range(HEADS):
        cols = slice(h * 128, (h + 1) * 128)
        send_kv[h, 0:32, :] = k_ref[:, cols]
        send_q[h] = q_ref[:, cols]
        vp = jnp.dot(v_ref[:, cols], w_ref[cols, :], preferred_element_type=F32)
        send_kv[h, 32:48, :] = jnp.concatenate([vp[0:16], vp[16:32]], axis=1).astype(BF16)

    pl.semaphore_wait(barrier, HEADS - 1 + 3 + NZ)

    def send_keys(i, carry):
        zz, yy = to_plane(i // 4), (y + i % 4) % 4
        pltpu.make_async_remote_copy(
            src_ref=send_kv.at[zz * 4 + yy],
            dst_ref=rkv.at[z, core, x, y],
            send_sem=s_kv, recv_sem=r_kv.at[z],
            device_id=group(yy, zz), device_id_type=MESH,
        ).start()
        return carry

    def send_queries(i, carry):
        zz, yy = to_plane(i // 4), (y + i % 4) % 4
        pltpu.make_async_remote_copy(
            src_ref=send_q.at[zz * 4 + yy],
            dst_ref=rq.at[z, y],
            send_sem=s_q, recv_sem=r_q.at[z],
            device_id=group(yy, zz), device_id_type=MESH,
        ).start()
        return carry

    pltpu.make_async_copy(send_kv.at[z * 4 + y], rkv.at[z, core, x, y], r_kv.at[z]).start()
    lax.fori_loop(1, HEADS, send_keys, 0)
    pltpu.make_async_copy(send_q.at[z * 4 + y], rq.at[z, y], r_q.at[z]).start()
    lax.fori_loop(1, HEADS, send_queries, 0)

    pieces = []
    for hf in range(2):
        for pr in range(2):
            for pc in range(2):
                pieces.append(noisy_ref[pr, pl.ds(hf * 16 + pc, 8, stride=2), :])
    noisy = jnp.concatenate(pieces, axis=1)

    def wait_recv(ref, sem):
        pltpu.make_async_remote_copy(
            src_ref=ref, dst_ref=ref, send_sem=s_kv, recv_sem=sem,
            device_id=sibling, device_id_type=MESH,
        ).wait_recv()

    def wait_send(ref, sem):
        pltpu.make_async_remote_copy(
            src_ref=ref, dst_ref=ref, send_sem=sem, recv_sem=r_core.at[0],
            device_id=sibling, device_id_type=MESH,
        ).wait_send()

    xl, xr, xo = (x + 3) % NX, (x + 1) % NX, (x + 2) % NX

    def spread(i, carry):
        @pl.when(i < NZ)
        def _():
            zs = from_plane(i)
            own = rkv.at[zs, core, x]
            wait_recv(own, r_kv.at[zs])
            pltpu.make_async_remote_copy(
                src_ref=own, dst_ref=own, send_sem=s_b1, recv_sem=r_b1.at[zs, 0],
                device_id=right, device_id_type=MESH,
            ).start()
            pltpu.make_async_remote_copy(
                src_ref=own, dst_ref=own, send_sem=s_b1, recv_sem=r_b1.at[zs, 1],
                device_id=left, device_id_type=MESH,
            ).start()

        @pl.when((i >= 1) & (i < NZ + 1))
        def _():
            zs = from_plane(i - 1)
            wait_recv(rkv.at[zs, core, xl], r_b1.at[zs, 0])
            first = rkv.at[zs, core, xl, pl.ds(0, 2)]
            pltpu.make_async_remote_copy(
                src_ref=first, dst_ref=first, send_sem=s_b2, recv_sem=r_b2.at[zs, 0],
                device_id=right, device_id_type=MESH,
            ).start()
            wait_recv(rkv.at[zs, core, xr], r_b1.at[zs, 1])
            second = rkv.at[zs, core, xr, pl.ds(2, 2)]
            pltpu.make_async_remote_copy(
                src_ref=second, dst_ref=second, send_sem=s_b2, recv_sem=r_b2.at[zs, 1],
                device_id=left, device_id_type=MESH,
            ).start()

        @pl.when((i >= 2) & (i < NZ + 2))
        def _():
            zs = from_plane(i - 2)
            wait_recv(rkv.at[zs, core, xo, pl.ds(0, 2)], r_b2.at[zs, 0])
            wait_recv(rkv.at[zs, core, xo, pl.ds(2, 2)], r_b2.at[zs, 1])
            pltpu.make_async_remote_copy(
                src_ref=rkv.at[zs, core], dst_ref=rkv.at[zs, core],
                send_sem=s_core, recv_sem=r_core.at[zs],
                device_id=sibling, device_id_type=MESH,
            ).start()

        @pl.when(i >= 3)
        def _():
            zs = from_plane(i - 3)
            wait_recv(rkv.at[zs, 1 - core], r_core.at[zs])
            packed = rkv[zs, :, :, :, 32:48, :].reshape(512, 128).astype(F32)
            turned = packed.T.astype(BF16)
            vt[zs, 0:64, 0:512] = turned[0:64]
            vt[zs, 0:64, 512:1024] = turned[64:128]
            vt[zs, 64:V_ROWS, :] = jnp.ones((V_ROWS - 64, 1024), BF16)

        return carry

    lax.fori_loop(0, NZ + 3, spread, 0)

    coefficient = jnp.where(cfg == 0, guide_scale, 1.0 - guide_scale).astype(F32)

    def combine(j):
        for t in range(1, 4):
            yy = (y + t) % 4
            wait_recv(c1r.at[j, yy], r_c1.at[j, yy])
        total = c1s[j, y].astype(F32)
        for t in range(1, 4):
            total = total + c1r[j, (y + t) % 4].astype(F32)
        c2s[j] = total.reshape(2, 2, 8, 128)
        for s in range(2):
            zz = from_plane(2 * j + s)
            for t in range(2):
                cc = (cfg + t) % 2
                mine = (zz == z) & (cc == cfg)

                @pl.when(mine)
                def _():
                    c2r[cfg * NZ + z] = c2s[j, s, cc]

                @pl.when(jnp.logical_not(mine))
                def _():
                    pltpu.make_async_remote_copy(
                        src_ref=c2s.at[j, s, cc], dst_ref=c2r.at[cfg * NZ + z],
                        send_sem=s_c2, recv_sem=r_c2.at[cfg * NZ + z],
                        device_id=(seq, zz * 2 + core, cc), device_id_type=MESH,
                    ).start()

    def attend(j, carry):
        za, zb = from_plane(2 * j), from_plane(2 * j + 1)
        wait_recv(rq.at[za], r_q.at[za])
        wait_recv(rq.at[zb], r_q.at[zb])
        query = jnp.concatenate([rq[za].reshape(128, 128), rq[zb].reshape(128, 128)], axis=0)

        def block(zc, state):
            largest, acc = state
            for part in range(2):
                keys = rkv[zc, :, :, :, 16 * part:16 * part + 16, :].reshape(512, 128)
                scores = lax.dot_general(
                    keys, query, (((1,), (1,)), ((), ())), preferred_element_type=F32
                ) * LOG_SCALE
                fresh = jnp.maximum(largest, jnp.max(scores, axis=0, keepdims=True))
                factor = jnp.exp2(largest - fresh)
                probs = jnp.exp2(scores - fresh).astype(BF16)
                mixed = jnp.dot(
                    vt[zc, :, 512 * part:512 * part + 512], probs, preferred_element_type=F32
                )
                acc = acc * factor + mixed
                largest = fresh
            return largest, acc

        largest, acc = lax.fori_loop(
            0, NZ, block,
            (jnp.full((1, 256), -1e30, F32), jnp.zeros((V_ROWS, 256), F32)),
        )
        out = acc[0:64] * (coefficient / acc[64:65])
        out = out.T.reshape(16, 2, 8, 64)
        out = jnp.concatenate([out[:, 0], out[:, 1]], axis=2)
        out = out.reshape(2, 4, 16, 128).astype(BF16)
        for yy in range(4):
            c1s[j, yy] = jnp.concatenate([out[0, yy], out[1, yy]], axis=0)
        for t in range(1, 4):
            yy = (y + t) % 4
            pltpu.make_async_remote_copy(
                src_ref=c1s.at[j, yy], dst_ref=c1r.at[j, y],
                send_sem=s_c1, recv_sem=r_c1.at[j, y],
                device_id=group(yy, z), device_id_type=MESH,
            ).start()

        @pl.when(j >= 1)
        def _():
            combine(j - 1)

        return carry

    lax.fori_loop(0, 4, attend, 0)
    combine(3)

    def wait_sum(i, carry):
        @pl.when(i != cfg * NZ + z)
        def _():
            wait_recv(c2r.at[i], r_c2.at[i])

        return carry

    lax.fori_loop(0, 2 * NZ, wait_sum, 0)
    clean = noisy - level_ref[0] * jnp.sum(c2r[...], axis=0)
    halo[0, 1, 0] = clean

    def neighbours(act):
        for a in range(3):
            for dr in range(-1, 2):
                for dc in range(2):
                    if (a, dr, dc) != (0, 0, 0):
                        act(a, dr, dc)

    def send_tile(a, dr, dc):
        @pl.when((seq + a < NX * NY) & (blk + dr >= 0) & (blk + dr < 2 * NZ))
        def _():
            pltpu.make_async_remote_copy(
                src_ref=halo.at[0, 1, 0], dst_ref=halo.at[a, 1 - dr, dc],
                send_sem=s_halo.at[a, 1 - dr, dc], recv_sem=r_halo.at[a, 1 - dr, dc],
                device_id=(seq + a, blk + dr, (cfg + dc) % 2), device_id_type=MESH,
            ).start()

    neighbours(send_tile)

    for hf in range(2):
        for pr in range(2):
            for pc in range(2):
                at = hf * 64 + pr * 32 + pc * 16
                clean_ref[pr, pl.ds(hf * 16 + pc, 8, stride=2), :] = clean[:, at:at + 16]

    def wait_tile(a, dr, dc):
        @pl.when((seq - a >= 0) & (blk + dr >= 0) & (blk + dr < 2 * NZ))
        def _():
            wait_recv(halo.at[a, 1 + dr, dc], r_halo.at[a, 1 + dr, dc])

    neighbours(wait_tile)

    for a in range(3):
        for row, (tile, pr) in enumerate(((0, 1), (1, 0), (1, 1), (2, 0))):
            near = halo[a, tile, 0]
            for hf in range(2):
                for pc in range(2):
                    at = hf * 64 + pr * 32 + pc * 16
                    ext[a, row, pl.ds(1 + hf * 16 + pc, 8, stride=2), :] = near[:, at:at + 16]
            far = halo[a, tile, 1]
            before = far[7:8, 64 + pr * 32 + 16:64 + pr * 32 + 32]
            after = far[0:1, pr * 32:pr * 32 + 16]
            ext[a, row, 0:1, :] = jnp.where(cfg == 1, before, 0.0)
            ext[a, row, 33:34, :] = jnp.where(cfg == 0, after, 0.0)

    tap = 0
    for a in range(3):
        for i in range(3):
            for j in range(3):
                window = ext[2 - a, i:i + 2, j:j + 32, :]
                patches[:, 16 * tap:16 * tap + 16] = window.reshape(64, 16)
                tap += 1
    conv = jnp.dot(patches[...].astype(BF16), cw_ref[...], preferred_element_type=F32)
    normed = conv * lax.rsqrt(jnp.mean(conv * conv, axis=1, keepdims=True) + norm_eps)
    decoded_ref[...] = (normed / (1.0 + jnp.exp(-normed))).astype(BF16)

    wait_send(send_kv.at[pl.ds(0, HEADS - 1)], s_kv)
    wait_send(send_q.at[pl.ds(0, HEADS - 1)], s_q)
    wait_send(rkv.at[pl.ds(0, 2)], s_b1)
    wait_send(rkv.at[pl.ds(0, 1)], s_b2)
    wait_send(rkv.at[pl.ds(0, 4)], s_core)
    wait_send(c1s.at[:, pl.ds(0, 3)], s_c1)
    wait_send(c2r.at[pl.ds(0, 2 * NZ - 1)], s_c2)

    def wait_sent(a, dr, dc):
        @pl.when((seq + a < NX * NY) & (blk + dr >= 0) & (blk + dr < 2 * NZ))
        def _():
            wait_send(halo.at[0, 1, 0], s_halo.at[a, 1 - dr, dc])

    neighbours(wait_sent)


def local(queries, keys, values, head_weight, noisy_latent, noise_level, conv_weight):
    vmem = pl.BlockSpec(memory_space=pltpu.VMEM)
    smem = pl.BlockSpec(memory_space=pltpu.SMEM)
    dma = pltpu.SemaphoreType.DMA
    clean, decoded = pl.pallas_call(
        kernel,
        out_shape=(
            jax.ShapeDtypeStruct((2, 32, 16), F32),
            jax.ShapeDtypeStruct((64, 384), BF16),
        ),
        in_specs=[vmem, vmem, vmem, vmem, vmem, smem, vmem],
        out_specs=(vmem, vmem),
        scratch_shapes=[
            pltpu.VMEM((HEADS, KV_ROWS, 128), BF16),
            pltpu.VMEM((HEADS, ROWS, 128), BF16),
            pltpu.VMEM((NZ, 2, NX, NY, KV_ROWS, 128), BF16),
            pltpu.VMEM((NZ, NY, ROWS, 128), BF16),
            pltpu.VMEM((NZ, V_ROWS, 1024), BF16),
            pltpu.VMEM((4, NY, 32, 128), BF16),
            pltpu.VMEM((4, NY, 32, 128), BF16),
            pltpu.VMEM((4, 2, 2, 8, 128), F32),
            pltpu.VMEM((2 * NZ, 8, 128), F32),
            pltpu.VMEM((3, 3, 2, 8, 128), F32),
            pltpu.VMEM((3, 4, 40, 16), F32),
            pltpu.VMEM((64, 432), F32),
            pltpu.VMEM((8, 128), F32),
            dma, dma, dma((NZ,)), dma((NZ,)),
            dma, dma((NZ, 2)), dma, dma((NZ, 2)), dma, dma((NZ,)),
            dma, dma((4, NY)), dma, dma((2 * NZ,)), dma((3, 3, 2)), dma((3, 3, 2)),
        ],
        compiler_params=pltpu.CompilerParams(
            collective_id=0, has_side_effects=True, vmem_limit_bytes=40 * 1024 * 1024
        ),
        name="denoise",
    )(
        queries[0], keys[0], values[0], head_weight, noisy_latent[0], noise_level,
        conv_weight.reshape(432, 384),
    )
    return clean[None], decoded.reshape(1, 2, 32, 384)


def solution(mesh):
    in_specs = (
        P("cfg", ("seq", "blk"), None),
        P("cfg", ("seq", "blk"), None),
        P("cfg", ("seq", "blk"), None),
        P(),
        P("seq", "blk", "cfg", None),
        P(),
        P(),
    )
    out_specs = (P("seq", "blk", "cfg", None), P("seq", "blk", "cfg", None))
    return jax.shard_map(local, mesh=mesh, in_specs=in_specs, out_specs=out_specs, check_vma=False)
```

time: 446 us -> 112 us (0.25)
  the two profiles are of different devices: /device:TPU:24 before, /device:TPU:9 now
where the time goes in v1:
time: 112 us
  Pallas kernels  107 us (96%)
  local copies, waits for them, and re-layouts  3.71 us (3%)
  between operations  1.34 us (1%)
    pallas_call x1, Pallas kernels, local(): pl.pallas_call(kernel, out_shape=(jax.ShapeDtypeStruct((2, 32, 16), F32),...  107 us
    unnamed x12, local copies, waits for them, and re-layouts  3.71 us

profile of v1, /device:TPU:9, one launch (start us, length us, event | category | flops | bytes accessed | tf_op | source)
XLA Modules:
  0.0 111.8 jit_solution(16330611040928722452)
XLA Ops:
  1.3 0.8 copy.9
  2.1 0.0 copy-start
  2.1 0.0 copy-start.1
  2.1 0.0 copy-start.2
  2.1 0.0 copy-start.3
  2.1 1.6 %copy.10.w_ref = bf16[4096,64]{1,0:T(8,128)(2,1)S(1)} copy(bf16[4096,64]{0,1:T(8,128)(2,1)} %param.10) | data formatting | bytes 1048576 | tf_op args[3]
  3.7 0.0 copy-done
  3.7 0.0 copy-done.1
  3.7 0.0 copy-done.2
  3.7 0.0 copy-done.3
  3.7 106.8 %denoise.1 = (f32[2,32,16]{2,1,0:T(8,128)S(1)}, bf16[64,384]{1,0:T(8,128)(2,1)S(1)}) custom-call(bf16[32,4096]{1,0:T(8,128)(2,1)S(1)} %bitcast.8, bf16[32,4096]{1,0:T(8,128)(2,1)S(1)} %bitcast.9, bf16[32,4096]{1,0:T(8,128)(2,1)S(1)} %bitcast.10, bf16[4096,64]{1,0:T(8,128)(2,1)S(1)} %copy.10.w_ref, f32[2,32,16]{2,1,0:T(8,128)S(1)} %bitcast.11, ...), custom_call_target="tpu_custom_call" | custom-call | tf_op jit(solution)/shard_map/denoise/pallas_call | solution.py:349
  110.5 0.7 copy.11
  111.2 0.6 copy.14
Async XLA Ops:
  2.1 1.6 %copy-start = (bf16[3,3,3,16,384]{4,3,2,1,0:T(8,128)(2,1)S(1)}, bf16[3,3,3,16,384]{4,3,2,1,0:T(8,128)(2,1)}, u32[]{:S(2)}) copy-start(bf16[3,3,3,16,384]{4,3,2,1,0:T(8,128)(2,1)} %param.13) | copy-start | bytes 995332
  2.1 1.6 %copy-start.1 = (bf16[1,32,4096]{2,1,0:T(8,128)(2,1)S(1)}, bf16[1,32,4096]{2,1,0:T(8,128)(2,1)}, u32[]{:S(2)}) copy-start(bf16[1,32,4096]{2,1,0:T(8,128)(2,1)} %param.7) | copy-start | bytes 786436
  2.1 1.7 %copy-start.2 = (bf16[1,32,4096]{2,1,0:T(8,128)(2,1)S(1)}, bf16[1,32,4096]{2,1,0:T(8,128)(2,1)}, u32[]{:S(2)}) copy-start(bf16[1,32,4096]{2,1,0:T(8,128)(2,1)} %param.8) | copy-start | bytes 786436
  2.1 1.7 %copy-start.3 = (bf16[1,32,4096]{2,1,0:T(8,128)(2,1)S(1)}, bf16[1,32,4096]{2,1,0:T(8,128)(2,1)}, u32[]{:S(2)}) copy-start(bf16[1,32,4096]{2,1,0:T(8,128)(2,1)} %param.9) | copy-start | bytes 786436

commit v2 on v1

v2 whole, which is shorter than its diff:
```python
import jax
import jax.numpy as jnp
from jax import lax
from jax.experimental import pallas as pl
from jax.experimental.pallas import tpu as pltpu
from jax.sharding import PartitionSpec as P

F32 = jnp.float32
BF16 = jnp.bfloat16
MESH = pl.DeviceIdType.MESH

guide_scale = 5.0
norm_eps = 1e-06
LOG_SCALE = float(128 ** (-0.5) * 1.4426950408889634)

NX = 4
NY = 4
NZ = 8
HEADS = 32
ROWS = 32
KV_ROWS = 48
V_ROWS = 80
TILE = 256


def kernel(
    q_hbm, k_hbm, v_hbm, wt_hbm, noisy_hbm, level_ref, cw_hbm,
    clean_ref, decoded_ref,
    q_ref, k_ref, v_ref, wt_ref, noisy_ref, cw_ref, s_load,
    send_kv, send_q, rkv, rq, vt, acc, top, c1s, c1r, c2s, c2r, noisy, halo, ext, patches, pixels,
    s_kv, s_q, r_kv, r_q, s_x, r_x, s_core, r_core,
    s_c1, r_c1, s_c2, r_c2, s_noisy, r_noisy, s_halo, r_halo,
):
    seq = lax.axis_index("seq")
    blk = lax.axis_index("blk")
    cfg = lax.axis_index("cfg")
    y, x = seq // NX, seq % NX
    z, core = blk // 2, blk % 2

    def from_plane(i):
        return (z + NZ - i) % NZ

    def group(yy, zz):
        return (yy * NX + x, zz * 2 + core, cfg)

    def target(i):
        yy, zz = (y + i % NY) % NY, (z + i // NY) % NZ
        return group(yy, zz), zz * NY + yy

    beside = [(y * NX + (x + t) % NX, blk, cfg) for t in (1, 3, 2)]
    sibling = (seq, z * 2 + 1 - core, cfg)
    partner = (seq, blk, 1 - cfg)

    def remote(src, dst, send_sem, recv_sem, device):
        return pltpu.make_async_remote_copy(
            src_ref=src, dst_ref=dst, send_sem=send_sem, recv_sem=recv_sem,
            device_id=device, device_id_type=MESH,
        )

    def wait_recv(ref, sem):
        remote(ref, ref, s_kv, sem, sibling).wait_recv()

    def wait_send(ref, sem):
        remote(ref, ref, sem, r_core.at[0], sibling).wait_send()

    loads = [
        pltpu.make_async_copy(src, dst, s_load.at[i])
        for i, (src, dst) in enumerate((
            (q_hbm, q_ref), (k_hbm, k_ref), (v_hbm, v_ref), (wt_hbm, wt_ref),
            (noisy_hbm, noisy_ref), (cw_hbm, cw_ref),
        ))
    ]
    for load in loads:
        load.start()

    halo[...] = jnp.zeros_like(halo)

    barrier = pltpu.get_barrier_semaphore()

    def greet(i, carry):
        pl.semaphore_signal(barrier, inc=1, device_id=target(i)[0], device_id_type=MESH)
        return carry

    lax.fori_loop(1, HEADS, greet, 0)
    for other in (*beside, sibling):
        pl.semaphore_signal(barrier, inc=1, device_id=other, device_id_type=MESH)

    def greet_branch(i, carry):
        pl.semaphore_signal(
            barrier, inc=1, device_id=(seq, i * 2 + core, 1 - cfg), device_id_type=MESH
        )
        return carry

    lax.fori_loop(0, NZ, greet_branch, 0)

    loads[0].wait()
    for h in range(HEADS):
        send_q[h] = q_ref[:, h * 128:(h + 1) * 128]

    loads[4].wait()
    for pr in range(2):
        pixels[pr] = noisy_ref[pr].T
    pieces = []
    for hf in range(2):
        for pr in range(2):
            for pc in range(2):
                pieces.append(pixels[pr, pl.ds(hf * 16 + pc, 8, stride=2), :])
    noisy[cfg] = jnp.concatenate(pieces, axis=1)

    pl.semaphore_wait(barrier, HEADS - 1 + NX + NZ)

    def send_queries(i, carry):
        device, head = target(i)
        remote(send_q.at[head], rq.at[y, z], s_q, r_q, device).start()
        return carry

    pltpu.make_async_copy(send_q.at[z * NY + y], rq.at[y, z], r_q).start()
    lax.fori_loop(1, HEADS, send_queries, 0)
    remote(noisy.at[cfg], noisy.at[cfg], s_noisy, r_noisy, partner).start()

    for load in loads[1:4]:
        load.wait()
    for h in range(HEADS):
        cols = slice(h * 128, (h + 1) * 128)
        send_kv[h, 0:32, :] = k_ref[:, cols]
        vp = lax.dot_general(
            v_ref[:, cols], wt_ref[:, cols], (((1,), (1,)), ((), ())), preferred_element_type=F32
        )
        send_kv[h, 32:48, :] = jnp.concatenate([vp[0:16], vp[16:32]], axis=1).astype(BF16)

    def send_keys(i, carry):
        device, head = target(i)
        remote(send_kv.at[head], rkv.at[z, core, x, y], s_kv, r_kv.at[z], device).start()
        return carry

    pltpu.make_async_copy(send_kv.at[z * NY + y], rkv.at[z, core, x, y], r_kv.at[z]).start()
    lax.fori_loop(1, HEADS, send_keys, 0)

    ext[...] = jnp.zeros_like(ext)
    acc[...] = jnp.zeros_like(acc)
    top[...] = jnp.full(top.shape, -1e30, F32)
    vt[:, 64:V_ROWS, :] = jnp.ones((NZ, V_ROWS - 64, 1024), BF16)

    coefficient = jnp.where(cfg == 0, guide_scale, 1.0 - guide_scale).astype(F32)

    def attend(zc):
        keys = jnp.concatenate(
            [rkv[zc, :, :, :, 16 * p:16 * p + 16, :].reshape(512, 128) for p in range(2)], axis=0
        )

        def scores_of(u):
            return lax.dot_general(
                keys, rq[(y + 1 + u) % NY].reshape(TILE, 128), (((1,), (1,)), ((), ())),
                preferred_element_type=F32,
            )

        scores = scores_of(0)
        for u in range(NY):
            yy = (y + 1 + u) % NY
            following = scores_of(u + 1) if u < NY - 1 else None
            before = top[yy, 0:1, :]
            fresh = jnp.maximum(before, jnp.max(scores, axis=0, keepdims=True) * LOG_SCALE)
            probs = jnp.exp2(scores * LOG_SCALE - fresh).astype(BF16)
            mixed = jnp.dot(vt[zc], probs, preferred_element_type=F32)
            acc[yy] = acc[yy] * jnp.exp2(before - fresh) + mixed
            top[yy, 0:1, :] = fresh
            scores = following

    def finish(u):
        yy = (y + 1 + u) % NY
        out = acc[yy, 0:64, :] * (coefficient / acc[yy, 64:65, :])
        out = out.T.reshape(2 * NZ, 2, 8, 64)
        out = jnp.concatenate([out[:, 0], out[:, 1]], axis=2)
        c1s[yy] = out.reshape(NZ, 16, 128).astype(BF16)
        if u < NY - 1:
            remote(c1s.at[yy], c1r.at[y], s_c1, r_c1.at[y], group(yy, z)).start()

    def step(n, carry):
        @pl.when(n < NZ)
        def _():
            zs = from_plane(n)
            own = rkv.at[zs, core, x]
            wait_recv(own, r_kv.at[zs])
            for device in beside:
                remote(own, own, s_x, r_x.at[zs, x], device).start()

        @pl.when((n >= 2) & (n < NZ + 2))
        def _():
            zs = from_plane(n - 2)
            for t in range(1, NX):
                xx = (x + t) % NX
                wait_recv(rkv.at[zs, core, xx], r_x.at[zs, xx])
            mine = rkv.at[zs, core]
            remote(mine, mine, s_core, r_core.at[zs], sibling).start()

        @pl.when(n == 3)
        def _():
            wait_recv(rq, r_q)

        @pl.when(n >= 3)
        def _():
            zs = from_plane(n - 3)
            wait_recv(rkv.at[zs, 1 - core], r_core.at[zs])
            packed = rkv[zs, :, :, :, 32:48, :].reshape(512, 128).astype(F32)
            turned = packed.T.astype(BF16)
            vt[zs, 0:64, 0:512] = turned[0:64]
            vt[zs, 0:64, 512:1024] = turned[64:128]
            attend(zs)

        return carry

    lax.fori_loop(0, NZ + 3, step, 0)
    for u in range(NY):
        finish(u)

    total = c1s[y].astype(F32)
    for t in range(1, NY):
        yy = (y + t) % NY
        wait_recv(c1r.at[yy], r_c1.at[yy])
        total = total + c1r[yy].astype(F32)
    c2s[...] = total.astype(BF16)
    c2r[cfg * NZ + z] = c2s[z]

    def send_sums(i, carry):
        zz, cc = (z + i // 2) % NZ, (cfg + i % 2) % 2
        remote(
            c2s.at[zz], c2r.at[cfg * NZ + z], s_c2, r_c2.at[cfg * NZ + z],
            (seq, zz * 2 + core, cc),
        ).start()
        return carry

    lax.fori_loop(1, 2 * NZ, send_sums, 0)
    wait_recv(noisy.at[1 - cfg], r_noisy)

    def wait_sum(i, carry):
        slot = (cfg * NZ + z + i) % (2 * NZ)
        wait_recv(c2r.at[slot], r_c2.at[slot])
        return carry

    lax.fori_loop(1, 2 * NZ, wait_sum, 0)
    velocity = jnp.sum(c2r[...].astype(F32), axis=0).reshape(2, 8, 128)
    halo[0, 1] = noisy[...] - level_ref[0] * velocity

    def neighbours(act):
        for a in range(3):
            for dr in range(-1, 2):
                if (a, dr) != (0, 0):
                    act(a, dr)

    def send_tile(a, dr):
        @pl.when((seq + a < NX * NY) & (blk + dr >= 0) & (blk + dr < 2 * NZ))
        def _():
            remote(
                halo.at[0, 1], halo.at[a, 1 - dr], s_halo.at[a, 1 - dr], r_halo.at[a, 1 - dr],
                (seq + a, blk + dr, cfg),
            ).start()

    neighbours(send_tile)
    loads[5].wait()

    def put_pixels(tile, pr, place):
        for hf in range(2):
            for pc in range(2):
                at = hf * 64 + pr * 32 + pc * 16
                place(hf * 16 + pc, tile[:, at:at + 16])

    clean = halo[0, 1, cfg]
    for pr in range(2):
        def place(start, values):
            pixels[pr, pl.ds(start, 8, stride=2), :] = values

        put_pixels(clean, pr, place)
        clean_ref[pr] = pixels[pr].T

    def wait_tile(a, dr):
        @pl.when((seq - a >= 0) & (blk + dr >= 0) & (blk + dr < 2 * NZ))
        def _():
            wait_recv(halo.at[a, 1 + dr], r_halo.at[a, 1 + dr])

    neighbours(wait_tile)

    for a in range(3):
        for row, (tile, pr) in enumerate(((0, 1), (1, 0), (1, 1), (2, 0))):
            def place(start, values):
                ext[a, row, pl.ds(1 + start, 8, stride=2), :] = values

            put_pixels(halo[a, tile, cfg], pr, place)
            far = halo[a, tile, 1 - cfg]
            before = far[7:8, 64 + pr * 32 + 16:64 + pr * 32 + 32]
            after = far[0:1, pr * 32:pr * 32 + 16]
            ext[a, row, 0:1, :] = jnp.where(cfg == 1, before, 0.0)
            ext[a, row, 33:34, :] = jnp.where(cfg == 0, after, 0.0)

    tap = 0
    for a in range(3):
        for i in range(3):
            for j in range(3):
                window = ext[2 - a, i:i + 2, j:j + 32, :]
                patches[:, 16 * tap:16 * tap + 16] = window.reshape(64, 16)
                tap += 1
    conv = jnp.dot(patches[...].astype(BF16), cw_ref[...], preferred_element_type=F32)
    normed = conv * lax.rsqrt(jnp.mean(conv * conv, axis=1, keepdims=True) + norm_eps)
    decoded_ref[...] = (normed / (1.0 + jnp.exp(-normed))).astype(BF16)

    wait_send(send_kv.at[pl.ds(0, HEADS - 1)], s_kv)
    wait_send(send_q.at[pl.ds(0, HEADS - 1)], s_q)
    wait_send(rkv.at[pl.ds(0, 3)], s_x)
    wait_send(rkv.at[pl.ds(0, 4)], s_core)
    wait_send(c1s.at[pl.ds(0, NY - 1)], s_c1)
    wait_send(c2r.at[pl.ds(0, 2 * NZ - 1)], s_c2)
    wait_send(noisy.at[0], s_noisy)

    def wait_sent(a, dr):
        @pl.when((seq + a < NX * NY) & (blk + dr >= 0) & (blk + dr < 2 * NZ))
        def _():
            wait_send(halo.at[0, 1], s_halo.at[a, 1 - dr])

    neighbours(wait_sent)


def local(queries, keys, values, head_weight, noisy_latent, noise_level, conv_weight):
    vmem = pl.BlockSpec(memory_space=pltpu.VMEM)
    hbm = pl.BlockSpec(memory_space=pltpu.HBM)
    smem = pl.BlockSpec(memory_space=pltpu.SMEM)
    dma = pltpu.SemaphoreType.DMA
    clean, decoded = pl.pallas_call(
        kernel,
        out_shape=(
            jax.ShapeDtypeStruct((2, 16, 32), F32),
            jax.ShapeDtypeStruct((64, 384), BF16),
        ),
        in_specs=[hbm, hbm, hbm, hbm, hbm, smem, hbm],
        out_specs=(vmem, vmem),
        scratch_shapes=[
            pltpu.VMEM((ROWS, HEADS * 128), BF16),
            pltpu.VMEM((ROWS, HEADS * 128), BF16),
            pltpu.VMEM((ROWS, HEADS * 128), BF16),
            pltpu.VMEM((64, HEADS * 128), BF16),
            pltpu.VMEM((2, 16, 32), F32),
            pltpu.VMEM((432, 384), BF16),
            dma((6,)),
            pltpu.VMEM((HEADS, KV_ROWS, 128), BF16),
            pltpu.VMEM((HEADS, ROWS, 128), BF16),
            pltpu.VMEM((NZ, 2, NX, NY, KV_ROWS, 128), BF16),
            pltpu.VMEM((NY, NZ, ROWS, 128), BF16),
            pltpu.VMEM((NZ, V_ROWS, 1024), BF16),
            pltpu.VMEM((NY, V_ROWS, TILE), F32),
            pltpu.VMEM((NY, 8, TILE), F32),
            pltpu.VMEM((NY, NZ, 16, 128), BF16),
            pltpu.VMEM((NY, NZ, 16, 128), BF16),
            pltpu.VMEM((NZ, 16, 128), BF16),
            pltpu.VMEM((2 * NZ, 16, 128), BF16),
            pltpu.VMEM((2, 8, 128), F32),
            pltpu.VMEM((3, 3, 2, 8, 128), F32),
            pltpu.VMEM((3, 4, 40, 16), F32),
            pltpu.VMEM((64, 432), F32),
            pltpu.VMEM((2, 32, 16), F32),
            dma, dma, dma((NZ,)), dma,
            dma, dma((NZ, NX)), dma, dma((NZ,)),
            dma, dma((NY,)), dma, dma((2 * NZ,)), dma, dma, dma((3, 3)), dma((3, 3)),
        ],
        compiler_params=pltpu.CompilerParams(
            collective_id=0, has_side_effects=True, vmem_limit_bytes=55142 * 1024
        ),
        name="denoise",
    )(
        queries[0], keys[0], values[0], head_weight.T,
        noisy_latent[0].transpose(0, 2, 1), noise_level, conv_weight.reshape(432, 384),
    )
    return clean.transpose(0, 2, 1)[None], decoded.reshape(1, 2, 32, 384)


def solution(mesh):
    in_specs = (
        P("cfg", ("seq", "blk"), None),
        P("cfg", ("seq", "blk"), None),
        P("cfg", ("seq", "blk"), None),
        P(),
        P("seq", "blk", "cfg", None),
        P(),
        P(),
    )
    out_specs = (P("seq", "blk", "cfg", None), P("seq", "blk", "cfg", None))
    return jax.shard_map(local, mesh=mesh, in_specs=in_specs, out_specs=out_specs, check_vma=False)
```

time: 112 us -> 86.6 us (0.77)
  Pallas kernels: 107 us -> 83.2 us
  local copies, waits for them, and re-layouts: 3.71 us -> 1.94 us
    pallas_call x1, Pallas kernels: 107 us -> 83.2 us  [local(): pl.pallas_call(kernel, out_shape=(jax.ShapeDtypeStruct((2, 16, 32), F32),...]
    unnamed x12 -> x4, local copies, waits for them, and re-layouts: 3.71 us -> 1.94 us
where the time goes in v2:
time: 86.6 us; the launch traced here: 86.5 us
  Pallas kernels  83.2 us (96%)
  local copies, waits for them, and re-layouts  1.94 us (2%)
  between operations  1.29 us (1%)
    pallas_call x1, Pallas kernels, local(): pl.pallas_call(kernel, out_shape=(jax.ShapeDtypeStruct((2, 16, 32), F32),...  83.2 us
    unnamed x4, local copies, waits for them, and re-layouts  1.94 us

profile of v2, /device:TPU:9, one launch (start us, length us, event | category | flops | bytes accessed | tf_op | source)
XLA Modules:
  0.0 86.5 jit_solution(2647794076229692871)
XLA Ops:
  1.3 0.0 copy-start
  1.3 0.7 copy-done
  2.0 83.2 %denoise.1 = (f32[2,16,32]{2,1,0:T(8,128)S(1)}, bf16[64,384]{1,0:T(8,128)(2,1)S(1)}) custom-call(bf16[32,4096]{1,0:T(8,128)(2,1)} %bitcast.17, bf16[32,4096]{1,0:T(8,128)(2,1)} %bitcast.18, bf16[32,4096]{1,0:T(8,128)(2,1)} %bitcast.19, bf16[64,4096]{1,0:T(8,128)(2,1)} %bitcast.15, f32[2,16,32]{2,1,0:T(8,128)S(1)} %bitcast.13, f32[1]{0:T(128)S(6)} %copy.11.level_ref, ...), custom_call_target="tpu_custom_call" | custom-call | tf_op jit(solution)/shard_map/denoise/pallas_call | solution.py:326
  85.2 0.6 copy.12
  85.8 0.6 copy.13
Async XLA Ops:
  1.3 0.7 copy-start

commit v3 on v2

--- a/solution.py
+++ b/solution.py
@@ -21,6 +21,10 @@
 KV_ROWS = 48
 V_ROWS = 80
 TILE = 256
+TILES = 4
+UNITS = 8
+LATE_STEP = 5
+EARLY = 1
 
 
 def kernel(
@@ -111,11 +115,12 @@
 
     def send_queries(i, carry):
         device, head = target(i)
-        remote(send_q.at[head], rq.at[y, z], s_q, r_q, device).start()
-        return carry
-
-    pltpu.make_async_copy(send_q.at[z * NY + y], rq.at[y, z], r_q).start()
-    lax.fori_loop(1, HEADS, send_queries, 0)
+        at = i // NY
+        remote(send_q.at[head], rq.at[at, y], s_q, r_q.at[at // 2], device).start()
+        return carry
+
+    pltpu.make_async_copy(send_q.at[z * NY + y], rq.at[0, y], r_q.at[0]).start()
+    lax.fori_loop(1, 2 * EARLY * NY, send_queries, 0)
     remote(noisy.at[cfg], noisy.at[cfg], s_noisy, r_noisy, partner).start()
 
     for load in loads[1:4]:
@@ -143,37 +148,85 @@
 
     coefficient = jnp.where(cfg == 0, guide_scale, 1.0 - guide_scale).astype(F32)
 
-    def attend(zc):
-        keys = jnp.concatenate(
-            [rkv[zc, :, :, :, 16 * p:16 * p + 16, :].reshape(512, 128) for p in range(2)], axis=0
-        )
-
-        def scores_of(u):
+    def attend(units):
+        def scores_of(zc, t):
+            keys = jnp.concatenate(
+                [rkv[zc, :, :, :, 16 * p:16 * p + 16, :].reshape(512, 128) for p in range(2)], axis=0
+            )
             return lax.dot_general(
-                keys, rq[(y + 1 + u) % NY].reshape(TILE, 128), (((1,), (1,)), ((), ())),
+                keys, rq[pl.ds(2 * t, 2)].reshape(TILE, 128), (((1,), (1,)), ((), ())),
                 preferred_element_type=F32,
             )
 
-        scores = scores_of(0)
-        for u in range(NY):
-            yy = (y + 1 + u) % NY
-            following = scores_of(u + 1) if u < NY - 1 else None
-            before = top[yy, 0:1, :]
+        scores = scores_of(*units[0])
+        for at, (zc, t) in enumerate(units):
+            following = scores_of(*units[at + 1]) if at + 1 < len(units) else None
+            before = top[t, 0:1, :]
             fresh = jnp.maximum(before, jnp.max(scores, axis=0, keepdims=True) * LOG_SCALE)
             probs = jnp.exp2(scores * LOG_SCALE - fresh).astype(BF16)
             mixed = jnp.dot(vt[zc], probs, preferred_element_type=F32)
-            acc[yy] = acc[yy] * jnp.exp2(before - fresh) + mixed
-            top[yy, 0:1, :] = fresh
+            acc[t] = acc[t] * jnp.exp2(before - fresh) + mixed
+            top[t, 0:1, :] = fresh
             scores = following
 
-    def finish(u):
-        yy = (y + 1 + u) % NY
-        out = acc[yy, 0:64, :] * (coefficient / acc[yy, 64:65, :])
-        out = out.T.reshape(2 * NZ, 2, 8, 64)
+    def finish(t):
+        out = acc[t, 0:64, :] * (coefficient / acc[t, 64:65, :])
+        out = out.T.reshape(16, 2, 8, 64)
         out = jnp.concatenate([out[:, 0], out[:, 1]], axis=2)
-        c1s[yy] = out.reshape(NZ, 16, 128).astype(BF16)
-        if u < NY - 1:
-            remote(c1s.at[yy], c1r.at[y], s_c1, r_c1.at[y], group(yy, z)).start()
+        out = out.reshape(2, NY, 16, 128).astype(BF16)
+        for yy in range(NY):
+            c1s[yy, pl.ds(2 * t, 2)] = out[:, yy]
+        for dy in range(1, NY):
+            yy = (y + dy) % NY
+            remote(
+                c1s.at[yy, pl.ds(2 * t, 2)], c1r.at[y, pl.ds(2 * t, 2)],
+                s_c1, r_c1.at[t, y], group(yy, z),
+            ).start()
+
+    def combine(t):
+        total = c1s[y, pl.ds(2 * t, 2)].astype(F32)
+        for dy in range(1, NY):
+            yy = (y + dy) % NY
+            wait_recv(c1r.at[yy, pl.ds(2 * t, 2)], r_c1.at[t, yy])
+            total = total + c1r[yy, pl.ds(2 * t, 2)].astype(F32)
+        c2s[pl.ds(2 * t, 2)] = total.astype(BF16)
+        for s in range(2):
+            i = 2 * t + s
+            zz = from_plane(i)
+
+            def send(cc):
+                remote(
+                    c2s.at[i], c2r.at[cfg * NZ + z], s_c2, r_c2.at[cfg * NZ + z],
+                    (seq, zz * 2 + core, cc),
+                ).start()
+
+            send(1 - cfg)
+
+            @pl.when(i > 0)
+            def _():
+                send(cfg)
+
+            @pl.when(i == 0)
+            def _():
+                c2r[cfg * NZ + z] = c2s[0]
+
+    def take(zs):
+        wait_recv(rkv.at[zs, 1 - core], r_core.at[zs])
+        packed = rkv[zs, :, :, :, 32:48, :].reshape(512, 128).astype(F32)
+        turned = packed.T.astype(BF16)
+        vt[zs, 0:64, 0:512] = turned[0:64]
+        vt[zs, 0:64, 512:1024] = turned[64:128]
+
+    def share(zs):
+        for t in range(1, NX):
+            xx = (x + t) % NX
+            wait_recv(rkv.at[zs, core, xx], r_x.at[zs, xx])
+        mine = rkv.at[zs, core]
+        remote(mine, mine, s_core, r_core.at[zs], sibling).start()
+
+    def wait_queries(tiles):
+        for t in tiles:
+            wait_recv(rq.at[pl.ds(2 * t, 2)], r_q.at[t])
 
     def step(n, carry):
         @pl.when(n < NZ)
@@ -184,52 +237,47 @@
             for device in beside:
                 remote(own, own, s_x, r_x.at[zs, x], device).start()
 
+        @pl.when((n >= LATE_STEP) & (n < LATE_STEP + TILES - EARLY))
+        def _():
+            first = (n - LATE_STEP + EARLY) * 2 * NY
+            lax.fori_loop(first, first + 2 * NY, send_queries, 0)
+
         @pl.when((n >= 2) & (n < NZ + 2))
         def _():
-            zs = from_plane(n - 2)
-            for t in range(1, NX):
-                xx = (x + t) % NX
-                wait_recv(rkv.at[zs, core, xx], r_x.at[zs, xx])
-            mine = rkv.at[zs, core]
-            remote(mine, mine, s_core, r_core.at[zs], sibling).start()
+            share(from_plane(n - 2))
 
         @pl.when(n == 3)
         def _():
-            wait_recv(rq, r_q)
+            wait_queries(range(EARLY))
 
         @pl.when(n >= 3)
         def _():
             zs = from_plane(n - 3)
-            wait_recv(rkv.at[zs, 1 - core], r_core.at[zs])
-            packed = rkv[zs, :, :, :, 32:48, :].reshape(512, 128).astype(F32)
-            turned = packed.T.astype(BF16)
-            vt[zs, 0:64, 0:512] = turned[0:64]
-            vt[zs, 0:64, 512:1024] = turned[64:128]
-            attend(zs)
+            take(zs)
+            attend([(zs, t) for t in range(EARLY)])
 
         return carry
 
     lax.fori_loop(0, NZ + 3, step, 0)
-    for u in range(NY):
-        finish(u)
-
-    total = c1s[y].astype(F32)
-    for t in range(1, NY):
-        yy = (y + t) % NY
-        wait_recv(c1r.at[yy], r_c1.at[yy])
-        total = total + c1r[yy].astype(F32)
-    c2s[...] = total.astype(BF16)
-    c2r[cfg * NZ + z] = c2s[z]
-
-    def send_sums(i, carry):
-        zz, cc = (z + i // 2) % NZ, (cfg + i % 2) % 2
-        remote(
-            c2s.at[zz], c2r.at[cfg * NZ + z], s_c2, r_c2.at[cfg * NZ + z],
-            (seq, zz * 2 + core, cc),
-        ).start()
-        return carry
-
-    lax.fori_loop(1, 2 * NZ, send_sums, 0)
+    for t in range(EARLY):
+        finish(t)
+
+    def late(t, carry):
+        wait_recv(rq.at[pl.ds(2 * t, 2)], r_q.at[t])
+
+        def chunks(k, inner):
+            attend([(UNITS * k + u, t) for u in range(UNITS)])
+            return inner
+
+        lax.fori_loop(0, NZ // UNITS, chunks, 0)
+        finish(t)
+        combine(t - EARLY)
+        return carry
+
+    lax.fori_loop(EARLY, TILES, late, 0)
+    for t in range(TILES - EARLY, TILES):
+        combine(t)
+
     wait_recv(noisy.at[1 - cfg], r_noisy)
 
     def wait_sum(i, carry):
@@ -342,10 +390,10 @@
             pltpu.VMEM((HEADS, KV_ROWS, 128), BF16),
             pltpu.VMEM((HEADS, ROWS, 128), BF16),
             pltpu.VMEM((NZ, 2, NX, NY, KV_ROWS, 128), BF16),
-            pltpu.VMEM((NY, NZ, ROWS, 128), BF16),
+            pltpu.VMEM((NZ, NY, ROWS, 128), BF16),
             pltpu.VMEM((NZ, V_ROWS, 1024), BF16),
-            pltpu.VMEM((NY, V_ROWS, TILE), F32),
-            pltpu.VMEM((NY, 8, TILE), F32),
+            pltpu.VMEM((TILES, V_ROWS, TILE), F32),
+            pltpu.VMEM((TILES, 8, TILE), F32),
             pltpu.VMEM((NY, NZ, 16, 128), BF16),
             pltpu.VMEM((NY, NZ, 16, 128), BF16),
             pltpu.VMEM((NZ, 16, 128), BF16),
@@ -355,9 +403,9 @@
             pltpu.VMEM((3, 4, 40, 16), F32),
             pltpu.VMEM((64, 432), F32),
             pltpu.VMEM((2, 32, 16), F32),
-            dma, dma, dma((NZ,)), dma,
+            dma, dma, dma((NZ,)), dma((TILES,)),
             dma, dma((NZ, NX)), dma, dma((NZ,)),
-            dma, dma((NY,)), dma, dma((2 * NZ,)), dma, dma, dma((3, 3)), dma((3, 3)),
+            dma, dma((TILES, NY)), dma, dma((2 * NZ,)), dma, dma, dma((3, 3)), dma((3, 3)),
         ],
         compiler_params=pltpu.CompilerParams(
             collective_id=0, has_side_effects=True, vmem_limit_bytes=55142 * 1024

time: 86.6 us -> 82.8 us (0.956)
  Pallas kernels: 83.2 us -> 79.4 us
    pallas_call x1, Pallas kernels: 83.2 us -> 79.4 us  [local(): pl.pallas_call(kernel, out_shape=(jax.ShapeDtypeStruct((2, 16, 32), F32),...]
where the time goes in v3:
time: 82.8 us; the launch traced here: 82.6 us
  Pallas kernels  79.4 us (96%)
  local copies, waits for them, and re-layouts  1.94 us (2%)
  between operations  1.29 us (2%)
    pallas_call x1, Pallas kernels, local(): pl.pallas_call(kernel, out_shape=(jax.ShapeDtypeStruct((2, 16, 32), F32),...  79.4 us
    unnamed x4, local copies, waits for them, and re-layouts  1.94 us

profile of v3, /device:TPU:9, one launch (start us, length us, event | category | flops | bytes accessed | tf_op | source)
XLA Modules:
  0.0 82.6 jit_solution(17856398886705298167)
XLA Ops:
  1.3 0.0 copy-start
  1.3 0.7 copy-done
  2.0 79.4 %denoise.1 = (f32[2,16,32]{2,1,0:T(8,128)S(1)}, bf16[64,384]{1,0:T(8,128)(2,1)S(1)}) custom-call(bf16[32,4096]{1,0:T(8,128)(2,1)} %bitcast.17, bf16[32,4096]{1,0:T(8,128)(2,1)} %bitcast.18, bf16[32,4096]{1,0:T(8,128)(2,1)} %bitcast.19, bf16[64,4096]{1,0:T(8,128)(2,1)} %bitcast.15, f32[2,16,32]{2,1,0:T(8,128)S(1)} %bitcast.13, f32[1]{0:T(128)S(6)} %copy.11.level_ref, ...), custom_call_target="tpu_custom_call" | custom-call | tf_op jit(solution)/shard_map/denoise/pallas_call | solution.py:374
  81.4 0.6 copy.12
  82.0 0.6 copy.13
Async XLA Ops:
  1.3 0.7 copy-start

commit v4 on v3

--- a/solution.py
+++ b/solution.py
@@ -22,7 +22,6 @@
 V_ROWS = 80
 TILE = 256
 TILES = 4
-UNITS = 8
 LATE_STEP = 5
 EARLY = 1
 
@@ -258,24 +257,23 @@
 
         return carry
 
-    lax.fori_loop(0, NZ + 3, step, 0)
-    for t in range(EARLY):
-        finish(t)
+    lax.fori_loop(0, NZ + 2, step, 0)
+
+    wait_queries([1])
+    attend([(from_plane(k), 1) for k in range(NZ - 1)])
+    take(from_plane(NZ - 1))
+    attend([(from_plane(NZ - 1), 0), (from_plane(NZ - 1), 1)])
+    finish(0)
+    finish(1)
 
     def late(t, carry):
         wait_recv(rq.at[pl.ds(2 * t, 2)], r_q.at[t])
-
-        def chunks(k, inner):
-            attend([(UNITS * k + u, t) for u in range(UNITS)])
-            return inner
-
-        lax.fori_loop(0, NZ // UNITS, chunks, 0)
+        attend([(k, t) for k in range(NZ)])
         finish(t)
-        combine(t - EARLY)
-        return carry
-
-    lax.fori_loop(EARLY, TILES, late, 0)
-    for t in range(TILES - EARLY, TILES):
+        return carry
+
+    lax.fori_loop(2, TILES, late, 0)
+    for t in range(TILES):
         combine(t)
 
     wait_recv(noisy.at[1 - cfg], r_noisy)

time: 82.8 us -> 82.6 us (level)
  no operation moved by 1% of the time
where the time goes in v4:
time: 82.6 us; the launch traced here: 82.5 us
  Pallas kernels  79.2 us (96%)
  local copies, waits for them, and re-layouts  1.94 us (2%)
  between operations  1.29 us (2%)
    pallas_call x1, Pallas kernels, local(): pl.pallas_call(kernel, out_shape=(jax.ShapeDtypeStruct((2, 16, 32), F32),...  79.2 us
    unnamed x4, local copies, waits for them, and re-layouts  1.94 us

profile of v4, /device:TPU:9, one launch (start us, length us, event | category | flops | bytes accessed | tf_op | source)
XLA Modules:
  0.0 82.5 jit_solution(5396807835308836750)
XLA Ops:
  1.3 0.0 copy-start
  1.3 0.7 copy-done
  2.0 79.2 %denoise.1 = (f32[2,16,32]{2,1,0:T(8,128)S(1)}, bf16[64,384]{1,0:T(8,128)(2,1)S(1)}) custom-call(bf16[32,4096]{1,0:T(8,128)(2,1)} %bitcast.17, bf16[32,4096]{1,0:T(8,128)(2,1)} %bitcast.18, bf16[32,4096]{1,0:T(8,128)(2,1)} %bitcast.19, bf16[64,4096]{1,0:T(8,128)(2,1)} %bitcast.15, f32[2,16,32]{2,1,0:T(8,128)S(1)} %bitcast.13, f32[1]{0:T(128)S(6)} %copy.11.level_ref, ...), custom_call_target="tpu_custom_call" | custom-call | tf_op jit(solution)/shard_map/denoise/pallas_call | solution.py:372
  81.2 0.6 copy.12
  81.8 0.6 copy.13
Async XLA Ops:
  1.3 0.7 copy-start
